TPU v7x, 32 devices: a whole 2x2x4 slice. The times are simulated.
32 devices in a mesh: dp: 2 (over x), seq: 16 (over z, y, core).
Axes of the slice: x: 2, y: 2, z: 4, core: 2. Of those that a mesh axis runs over, the one named last changes fastest.
Arguments:
- tokens: bfloat16 [2, 2048, 768], P('dp', 'seq'), may hold values from -6 to 6
- cotangent: bfloat16 [2, 2048, 768], P('dp', 'seq'), may hold values from -6 to 6
- mix_gain: float32 [2, 768], replicated, may hold values from 0.5 to 1.5
- in_proj: bfloat16 [2, 768, 2304], replicated, may hold values from -0.21875 to 0.21875
- short_taps: float32 [2, 3, 2304], replicated, may hold values from -3 to 3
- filter_first: float32 [2, 33, 64], replicated, may hold values from -1 to 1
- filter_middle: float32 [2, 64, 64], replicated, may hold values from -0.75 to 0.75
- filter_last: float32 [2, 64, 768], replicated, may hold values from -1 to 1
- filter_skip: float32 [2, 768], replicated, may hold values from -4 to 4
- decay_rates: float32 [2, 768], replicated, may hold values from 0.00024414062 to 0.03
- out_proj: bfloat16 [2, 768, 768], replicated, may hold values from -0.21875 to 0.21875
- mlp_gain: float32 [2, 768], replicated, may hold values from 0.5 to 1.5
- up_proj: bfloat16 [2, 768, 3072], replicated, may hold values from -0.21875 to 0.21875
- down_proj: bfloat16 [2, 3072, 768], replicated, may hold values from -0.109375 to 0.109375
Outputs:
- outputs: float32 [2, 2048, 768], P('dp', 'seq')
- grad_tokens: float32 [2, 2048, 768], P('dp', 'seq')
- grad_mix_gain: float32 [2, 768], replicated
- grad_in_proj: float32 [2, 768, 2304], P(None, 'seq', 'dp')
- grad_short_taps: float32 [2, 3, 2304], replicated
- grad_filter_first: float32 [2, 33, 64], replicated
- grad_filter_middle: float32 [2, 64, 64], replicated
- grad_filter_last: float32 [2, 64, 768], P(None, None, 'seq')
- grad_filter_skip: float32 [2, 768], P(None, 'seq')
- grad_out_proj: float32 [2, 768, 768], P(None, 'seq', 'dp')
- grad_mlp_gain: float32 [2, 768], replicated
- grad_up_proj: float32 [2, 768, 3072], P(None, 'seq', 'dp')
- grad_down_proj: float32 [2, 3072, 768], P(None, 'seq', 'dp')
All inputs are finite; a program needn't handle non-finite values.
Results may differ from a plain program's by a relative error of at most 0.023.
Values may be sent and summed in bfloat16 or wider, within the bound.
No kernel may reach another device: no remote copies, remote signals or barrier semaphores. Data moves between devices by JAX's collectives and lax.ppermute only.
A program may use at most 320 MiB of HBM per device.

v0:
```python
import math

import jax
import jax.numpy as jnp
from jax import lax
from jax.sharding import PartitionSpec as P

FEATS = 33
FFT_COLS = 512


HIGHEST = lax.Precision.HIGHEST
EPSILON = 1e-05


def from_behind(block, axis, distance):
    devices = range(lax.axis_size(axis))
    route = [(i - distance, i) for i in devices if i - distance in devices]
    return lax.ppermute(block, axis, route)


def high_einsum(form, left, right):
    return jnp.einsum(form, left, right, precision=HIGHEST)


def low_einsum(form, left, right):
    return jnp.einsum(form, left, right, preferred_element_type=jnp.float32)


def to_low(value):
    return lax.optimization_barrier(value.astype(jnp.bfloat16))


def angle_table(rows, columns, modulus):
    product = lax.broadcasted_iota(jnp.int32, (rows, columns), 0) * lax.broadcasted_iota(
        jnp.int32, (rows, columns), 1
    )
    angle = (product % modulus).astype(jnp.float32) * (2.0 * math.pi / modulus)
    return (jnp.cos(angle), jnp.sin(angle))


def transform_tables(length, columns):
    total = 2 * length
    rows = total // columns
    cos_rows, sin_rows = angle_table(rows, rows, rows)
    cos_columns, sin_columns = angle_table(columns, columns, columns)
    cos_turn, sin_turn = angle_table(rows, columns, total)
    return (cos_rows, sin_rows, cos_columns, sin_columns, cos_turn, sin_turn)


def forward_transform(signal, tables):
    cos_rows, sin_rows, cos_columns, sin_columns, cos_turn, sin_turn = tables
    channels, length = signal.shape
    rows, columns = cos_turn.shape
    padded = jnp.pad(signal, ((0, 0), (0, length))).reshape(channels, rows, columns)
    first_real = high_einsum("kq,cqp->ckp", cos_rows, padded)
    first_imag = -high_einsum("kq,cqp->ckp", sin_rows, padded)
    turned_real = first_real * cos_turn + first_imag * sin_turn
    turned_imag = first_imag * cos_turn - first_real * sin_turn
    spec_real = high_einsum("ckp,pj->ckj", turned_real, cos_columns) + high_einsum(
        "ckp,pj->ckj", turned_imag, sin_columns
    )
    spec_imag = high_einsum("ckp,pj->ckj", turned_imag, cos_columns) - high_einsum(
        "ckp,pj->ckj", turned_real, sin_columns
    )
    return (spec_real, spec_imag)


def inverse_transform(spec_real, spec_imag, tables):
    cos_rows, sin_rows, cos_columns, sin_columns, cos_turn, sin_turn = tables
    rows, columns = cos_turn.shape
    back_real = high_einsum("ckp,pj->ckj", spec_real, cos_columns) - high_einsum(
        "ckp,pj->ckj", spec_imag, sin_columns
    )
    back_imag = high_einsum("ckp,pj->ckj", spec_imag, cos_columns) + high_einsum(
        "ckp,pj->ckj", spec_real, sin_columns
    )
    turned_real = back_real * cos_turn - back_imag * sin_turn
    turned_imag = back_imag * cos_turn + back_real * sin_turn
    signal = high_einsum("qk,ckp->cqp", cos_rows, turned_real) - high_einsum(
        "qk,ckp->cqp", sin_rows, turned_imag
    )
    total = rows * columns
    return signal.reshape(signal.shape[0], total)[:, : total // 2] / total


def position_features(length):
    count = (FEATS - 1) // 2
    steps = lax.broadcasted_iota(jnp.int32, (count, length), 1)
    frequency = lax.broadcasted_iota(jnp.int32, (count, length), 0) + 1
    angle = (steps * frequency % length).astype(jnp.float32) * (2.0 * math.pi / length)
    ramp = lax.broadcasted_iota(jnp.int32, (1, length), 1).astype(jnp.float32) / length
    return jnp.concatenate([ramp, jnp.cos(angle), jnp.sin(angle)], axis=0)


def filter_forward(features, first, middle, last_columns, rate_columns, length):
    pre_one = high_einsum("fk,ft->kt", first, features)
    act_one = jnp.sin(pre_one)
    pre_two = high_einsum("kj,kt->jt", middle, act_one)
    act_two = jnp.sin(pre_two)
    raw = high_einsum("kc,kt->ct", last_columns, act_two)
    steps = lax.broadcasted_iota(jnp.int32, (1, length), 1).astype(jnp.float32)
    window = jnp.exp(-rate_columns[:, None] * steps) * jnp.sqrt(
        rate_columns[:, None] + 1.0 / length
    )
    return (raw * window, (pre_one, act_one, pre_two, act_two, window))


def filter_backward(d_response, features, middle, last_columns, kept):
    pre_one, act_one, pre_two, act_two, window = kept
    d_raw = d_response * window
    g_last = high_einsum("kt,ct->kc", act_two, d_raw)
    d_two = high_einsum("kc,ct->kt", last_columns, d_raw) * jnp.cos(pre_two)
    g_middle = high_einsum("kt,jt->kj", act_one, d_two)
    d_one = high_einsum("kj,jt->kt", middle, d_two) * jnp.cos(pre_one)
    g_first = high_einsum("ft,kt->fk", features, d_one)
    return (g_first, g_middle, g_last)


def normalize(state):
    centred = state - jnp.mean(state, axis=1, keepdims=True)
    scale = lax.rsqrt(jnp.mean(centred * centred, axis=1, keepdims=True) + EPSILON)
    return (centred * scale, scale)


def normalize_back(d_out, normed, scale, gain):
    d_normed = d_out * gain
    g_gain = jnp.sum(d_out * normed, axis=0)
    d_state = scale * (
        d_normed
        - jnp.mean(d_normed, axis=1, keepdims=True)
        - normed * jnp.mean(d_normed * normed, axis=1, keepdims=True)
    )
    return (d_state, g_gain)


def short_forward(extended, taps):
    length = extended.shape[-1] - 2
    return (
        taps[0] * extended[..., 2:]
        + taps[1] * extended[..., 1 : length + 1]
        + taps[2] * extended[..., :length]
    )


def short_backward(d_extended, taps):
    length = d_extended.shape[-1] - 2
    return (
        taps[0] * d_extended[..., :length]
        + taps[1] * d_extended[..., 1 : length + 1]
        + taps[2] * d_extended[..., 2:]
    )


def tap_grads(d_shorted, extended):
    length = d_shorted.shape[-1]
    return jnp.stack(
        [
            jnp.sum(d_shorted * extended[..., 2 - lag : 2 - lag + length], axis=-1)
            for lag in range(3)
        ]
    )


def long_forward(gated, filter_real, filter_imag, skip_columns, tables):
    signal = gated.astype(jnp.float32)
    sig_real, sig_imag = forward_transform(signal, tables)
    result = inverse_transform(
        sig_real * filter_real - sig_imag * filter_imag,
        sig_real * filter_imag + sig_imag * filter_real,
        tables,
    )
    return (result + skip_columns[:, None] * signal, (sig_real, sig_imag))


def long_backward(d_conv, gated, filter_real, filter_imag, skip_columns, signal_spec, tables):
    d_signal = d_conv.astype(jnp.float32)
    d_real, d_imag = forward_transform(d_signal, tables)
    sig_real, sig_imag = signal_spec
    d_gated = (
        inverse_transform(
            d_real * filter_real + d_imag * filter_imag,
            d_imag * filter_real - d_real * filter_imag,
            tables,
        )
        + skip_columns[:, None] * d_signal
    )
    d_response = inverse_transform(
        d_real * sig_real + d_imag * sig_imag, d_imag * sig_real - d_real * sig_imag, tables
    )
    g_skip = jnp.sum(d_signal * gated.astype(jnp.float32), axis=1)
    return (d_gated, d_response, g_skip)


def layer_forward(state, weights, setting):
    (
        mix_gain,
        in_proj,
        short_taps,
        first,
        middle,
        last,
        skip,
        rates,
        out_proj,
        mlp_gain,
        up_proj,
        down_proj,
    ) = weights
    features, tables, offset = setting
    rows, width = state.shape
    length = features.shape[1]
    channels = width // (length // rows)
    normed_mix, scale_mix = normalize(state)
    u_mix = to_low(normed_mix * mix_gain)
    projected = to_low(low_einsum("td,dc->ct", u_mix, in_proj)).reshape(3, width, rows)
    last_columns = lax.dynamic_slice_in_dim(last, offset, channels, 1)
    skip_columns = lax.dynamic_slice_in_dim(skip, offset, channels, 0)
    rate_columns = lax.dynamic_slice_in_dim(rates, offset, channels, 0)
    response, filter_kept = filter_forward(
        features, first, middle, last_columns, rate_columns, length
    )
    filter_real, filter_imag = forward_transform(response, tables)
    taps = short_taps.reshape(3, 3, width)
    edge = from_behind(projected[:, :, rows - 2 :], "seq", 1)
    extended = jnp.concatenate([edge, projected], axis=2).astype(jnp.float32)
    tap_use = taps[:, :, :, None]
    shorted = short_forward(extended, tap_use)
    gated_rows = to_low(shorted[2] * shorted[1])
    gated = lax.all_to_all(gated_rows, "seq", split_axis=0, concat_axis=1, tiled=True)
    conv, signal_spec = long_forward(gated, filter_real, filter_imag, skip_columns, tables)
    conv_low = to_low(conv)
    conv_here = lax.all_to_all(conv_low, "seq", split_axis=1, concat_axis=0, tiled=True)
    mixed = to_low(conv_here.astype(jnp.float32) * shorted[0])
    middle_state = state + low_einsum("ct,ce->te", mixed, out_proj)
    normed_mlp, scale_mlp = normalize(middle_state)
    u_mlp = to_low(normed_mlp * mlp_gain)
    hidden = low_einsum("td,df->tf", u_mlp, up_proj)
    active = to_low(jax.nn.gelu(hidden))
    result = middle_state + low_einsum("tf,fe->te", active, down_proj)
    kept = (
        normed_mix,
        scale_mix,
        u_mix,
        extended,
        shorted,
        gated,
        conv_here,
        mixed,
        filter_kept,
        filter_real,
        filter_imag,
        signal_spec,
        normed_mlp,
        scale_mlp,
        u_mlp,
        hidden,
        active,
        last_columns,
        skip_columns,
        tap_use,
    )
    return (result, kept)


def layer_backward(upstream, kept, weights, setting):
    (
        mix_gain,
        in_proj,
        short_taps,
        first,
        middle,
        last,
        skip,
        rates,
        out_proj,
        mlp_gain,
        up_proj,
        down_proj,
    ) = weights
    features, tables, offset = setting
    (
        normed_mix,
        scale_mix,
        u_mix,
        extended,
        shorted,
        gated,
        conv_here,
        mixed,
        filter_kept,
        filter_real,
        filter_imag,
        signal_spec,
        normed_mlp,
        scale_mlp,
        u_mlp,
        hidden,
        active,
        last_columns,
        skip_columns,
        tap_use,
    ) = kept
    rows, width = upstream.shape
    d_down = to_low(upstream)
    g_down = low_einsum("tf,te->fe", active, d_down)
    d_active = low_einsum("te,fe->tf", d_down, down_proj)
    d_hidden = to_low(jax.vjp(jax.nn.gelu, hidden)[1](d_active)[0])
    g_up = low_einsum("td,tf->df", u_mlp, d_hidden)
    d_u_mlp = low_einsum("tf,df->td", d_hidden, up_proj)
    d_middle, g_mlp_gain = normalize_back(d_u_mlp, normed_mlp, scale_mlp, mlp_gain)
    d_middle = d_middle + upstream
    d_branch = to_low(d_middle)
    g_out = low_einsum("ct,te->ce", mixed, d_branch)
    d_mixed = to_low(low_einsum("te,ce->ct", d_branch, out_proj))
    d_mixed_wide = d_mixed.astype(jnp.float32)
    d_conv_rows = to_low(d_mixed_wide * shorted[0])
    d_zero = d_mixed_wide * conv_here.astype(jnp.float32)
    d_conv = lax.all_to_all(d_conv_rows, "seq", split_axis=0, concat_axis=1, tiled=True)
    d_gated, d_response, g_skip = long_backward(
        d_conv, gated, filter_real, filter_imag, skip_columns, signal_spec, tables
    )
    d_gated_rows = lax.all_to_all(
        to_low(d_gated), "seq", split_axis=1, concat_axis=0, tiled=True
    ).astype(jnp.float32)
    d_shorted = jnp.stack([d_zero, d_gated_rows * shorted[2], d_gated_rows * shorted[1]])
    after = from_behind(d_shorted[:, :, :2], "seq", -1)
    d_extended = jnp.concatenate([d_shorted, after], axis=2)
    d_projected = to_low(short_backward(d_extended, tap_use))
    g_taps = tap_grads(d_shorted, extended)
    g_first, g_middle, g_last = filter_backward(
        d_response, features, middle, last_columns, filter_kept
    )
    d_flat = d_projected.reshape(3 * width, rows)
    g_in = low_einsum("td,ct->dc", u_mix, d_flat)
    d_u_mix = low_einsum("ct,dc->td", d_flat, in_proj)
    d_state, g_mix_gain = normalize_back(d_u_mix, normed_mix, scale_mix, mix_gain)
    d_state = d_state + d_middle
    large = (g_in, g_out, g_up, g_down)
    small = (g_mix_gain, g_taps.reshape(3, 3 * width), g_first, g_middle, g_mlp_gain)
    column_part = (g_last, g_skip)
    return (d_state, large, small, column_part)


def body(
    tokens,
    cotangent,
    mix_gain,
    in_proj,
    short_taps,
    filter_first,
    filter_middle,
    filter_last,
    filter_skip,
    decay_rates,
    out_proj,
    mlp_gain,
    up_proj,
    down_proj,
):
    rows = tokens.shape[1]
    width = tokens.shape[2]
    layer_count = mix_gain.shape[0]
    shards = lax.axis_size("seq")
    length = rows * shards
    offset = lax.axis_index("seq") * (width // shards)
    setting = (position_features(length), transform_tables(length, FFT_COLS), offset)
    stacks = (
        mix_gain,
        in_proj,
        short_taps,
        filter_first,
        filter_middle,
        filter_last,
        filter_skip,
        decay_rates,
        out_proj,
        mlp_gain,
        up_proj,
        down_proj,
    )
    state = tokens[0].astype(jnp.float32)
    kept_all = []
    for level in range(layer_count):
        weights = tuple((item[level] for item in stacks))
        state, kept = layer_forward(state, weights, setting)
        kept_all.append(kept)
    upstream = cotangent[0].astype(jnp.float32)
    large_all = [None] * layer_count
    small_all = [None] * layer_count
    column_all = [None] * layer_count
    for level in reversed(range(layer_count)):
        weights = tuple((item[level] for item in stacks))
        upstream, large, small, column_part = layer_backward(
            upstream, kept_all[level], weights, setting
        )
        large_all[level] = large
        small_all[level] = small
        column_all[level] = column_part
    stacked_large = [
        jnp.stack([large_all[level][member] for level in range(layer_count)]) for member in range(4)
    ]
    row_in, row_out, row_up, row_down = (
        lax.psum_scatter(stacked_large[0], "seq", scatter_dimension=1, tiled=True),
        lax.psum_scatter(stacked_large[1], "seq", scatter_dimension=1, tiled=True),
        lax.psum_scatter(stacked_large[2], "seq", scatter_dimension=1, tiled=True),
        lax.psum_scatter(stacked_large[3], "seq", scatter_dimension=1, tiled=True),
    )
    g_in, g_out, g_up, g_down = (
        lax.psum_scatter(row_in.astype(jnp.bfloat16), "dp", scatter_dimension=2, tiled=True).astype(
            jnp.float32
        ),
        lax.psum_scatter(
            row_out.astype(jnp.bfloat16), "dp", scatter_dimension=2, tiled=True
        ).astype(jnp.float32),
        lax.psum_scatter(row_up.astype(jnp.bfloat16), "dp", scatter_dimension=2, tiled=True).astype(
            jnp.float32
        ),
        lax.psum_scatter(
            row_down.astype(jnp.bfloat16), "dp", scatter_dimension=2, tiled=True
        ).astype(jnp.float32),
    )
    stacked_small = [
        jnp.stack([small_all[level][member] for level in range(layer_count)]) for member in range(5)
    ]
    g_mix_gain, g_taps, g_first, g_middle, g_mlp_gain = lax.psum(
        (stacked_small[0], stacked_small[1], stacked_small[2], stacked_small[3], stacked_small[4]),
        ("dp", "seq"),
    )
    stacked_last = jnp.stack([column_all[level][0] for level in range(layer_count)])
    stacked_skip = jnp.stack([column_all[level][1] for level in range(layer_count)])
    g_last, g_skip = lax.psum((stacked_last, stacked_skip), "dp")
    return (
        state[None],
        upstream[None],
        g_mix_gain,
        g_in,
        g_taps,
        g_first,
        g_middle,
        g_last,
        g_skip,
        g_out,
        g_mlp_gain,
        g_up,
        g_down,
    )


def solution(mesh):
    in_specs = (
        P("dp", "seq", None),
        P("dp", "seq", None),
        P(),
        P(),
        P(),
        P(),
        P(),
        P(),
        P(),
        P(),
        P(),
        P(),
        P(),
        P(),
    )
    out_specs = (
        P("dp", "seq", None),
        P("dp", "seq", None),
        P(),
        P(None, "seq", "dp"),
        P(),
        P(),
        P(),
        P(None, None, "seq"),
        P(None, "seq"),
        P(None, "seq", "dp"),
        P(),
        P(None, "seq", "dp"),
        P(None, "seq", "dp"),
    )
    return jax.shard_map(body, mesh=mesh, in_specs=in_specs, out_specs=out_specs, check_vma=False)
```

profile of v0, /device:TPU:0, one launch (start us, length us, event | category | flops | bytes accessed | tf_op | source)
XLA Modules:
  0.0 1127.7 jit_solution(12639330383834217753)
XLA Ops:
  36.0 6.4 fusion.168
  52.0 6.4 convolution_subtract_fusion.16
  58.5 6.3 fusion.152
  66.6 7.2 all-to-all-start
  73.9 7.9 convolution_add_fusion.10
  97.0 6.2 convolution_add_fusion.11
  103.2 6.9 multiply_subtract_fusion.9
  121.7 6.2 convolution_add_fusion.9
  142.2 7.9 convolution_subtract_fusion.12
  169.0 7.7 fusion.156
  186.2 7.8 convolution_add_fusion.7
  209.3 6.4 convolution_add_fusion.8
  215.7 6.9 multiply_subtract_fusion.6
  254.3 9.0 all-to-all-done.3
  284.6 12.9 %all_to_all.104 = bf16[16,48,128]{2,1,0:T(8,128)(2,1)S(1)} all-to-all(bf16[16,48,128]{2,1,0:T(8,128)(2,1)} %bitcast.651), channel_id=1, replica_groups=mesh['dp'=2,'seq'=16] {'seq'}, dimensions={0} | all-to-all | bytes 393216 | tf_op jit(solution)/shard_map/all_to_all | solution.py:319
  317.6 7.0 multiply_add_fusion.2
  342.0 6.2 convolution_subtract_fusion.8
  351.0 11.6 %all_to_all.105 = bf16[48,16,128]{2,0,1:T(8,128)(2,1)S(1)} all-to-all(bf16[48,16,128]{2,0,1:T(8,128)(2,1)S(1)} %copy_bitcast_fusion.5), channel_id=1, replica_groups=mesh['dp'=2,'seq'=16] {'seq'}, dimensions={1} | all-to-all | bytes 393216 | tf_op jit(solution)/shard_map/all_to_all | solution.py:323
  425.1 7.3 multiply_add_fusion.3
  459.4 15.0 %all_to_all.106 = bf16[48,16,128]{2,0,1:T(8,128)(2,1)S(1)} all-to-all(bf16[48,16,128]{2,0,1:T(8,128)(2,1)S(1)} %copy_bitcast_fusion.4), channel_id=1, replica_groups=mesh['dp'=2,'seq'=16] {'seq'}, dimensions={1} | all-to-all | bytes 393216 | tf_op jit(solution)/shard_map/all_to_all | solution.py:323
  491.4 11.0 pad_maximum_fusion.2
  506.4 8.6 pad_maximum_fusion.1
  519.1 9.5 pad_maximum_fusion
  564.1 7.0 fusion.128
  583.0 6.1 convolution_subtract_fusion.3
  605.9 43.9 %reduce-scatter.15.cloned.1.call-done = f32[2,48,2304]{2,1,0:T(8,128)} async-done(((f32[2,768,2304]{2,1,0:T(8,128)}), f32[2,48,2304]{2,1,0:T(8,128)}) %reduce-scatter.15.cloned.1.call-update) | async-done | bytes 884752 | tf_op jit(solution)/shard_map/reduce_scatter | solution.py:404
  656.2 194.2 %reduce-scatter.23.cloned.1.call-done = f32[2,192,768]{2,1,0:T(8,128)} async-done(((f32[2,3072,768]{2,1,0:T(8,128)}), f32[2,192,768]{2,1,0:T(8,128)}) %reduce-scatter.23.cloned.1.call-update) | async-done | bytes 1179664 | tf_op jit(solution)/shard_map/reduce_scatter | solution.py:407
  861.5 187.5 %reduce-scatter.19.cloned.1.call-done = f32[2,48,3072]{2,1,0:T(8,128)} async-done(((f32[2,768,3072]{2,1,0:T(8,128)}), f32[2,48,3072]{2,1,0:T(8,128)}) %reduce-scatter.19.cloned.1.call-update) | async-done | bytes 1179664 | tf_op jit(solution)/shard_map/reduce_scatter | solution.py:406
  1053.0 9.7 all-reduce.7
  1066.9 12.7 %reduce-scatter.25.cloned.1.call-done = bf16[1152,96]{1,0:T(8,128)(2,1)} async-done(((bf16[2304,96]{1,0:T(8,128)(2,1)}), bf16[1152,96]{1,0:T(8,128)(2,1)}) %reduce-scatter.25.cloned.1.call-update) | async-done | bytes 221200
  1082.3 14.9 %reduce-scatter.29.cloned.1.call-done = bf16[384,384]{1,0:T(8,128)(2,1)} async-done(((bf16[768,384]{1,0:T(8,128)(2,1)}), bf16[384,384]{1,0:T(8,128)(2,1)}) %reduce-scatter.29.cloned.1.call-update) | async-done | bytes 294928
  1100.0 15.4 %reduce-scatter.21.cloned.1.call-done = bf16[2,48,1536]{2,1,0:T(8,128)(2,1)} async-done(((bf16[2,48,3072]{2,1,0:T(8,128)(2,1)}), bf16[2,48,1536]{2,1,0:T(8,128)(2,1)}) %reduce-scatter.21.cloned.1.call-update) | async-done | bytes 294928 | tf_op jit(solution)/shard_map/reduce_scatter | solution.py:416
  (643 shorter events, 428.5 us)
Async XLA Ops:
  16.5 48.5 %collective-permute-start = (bf16[3,768,2]{1,2,0:T(2,128)(2,1)S(1)}, bf16[3,768,2]{1,2,0:T(2,128)(2,1)S(1)}, u32[]{:S(2)}, u32[]{:S(2)}) collective-permute-start(bf16[3,768,2]{1,2,0:T(2,128)(2,1)S(1)} %slice.262), channel_id=1, source_target_pairs={{0,1},{1,2},{2,3},{3,4},{4,5},{5,6},{6,7},{7,8},{8,9},{9,10},{10,1... | collective-permute-start | bytes 27656 | tf_op jit(solution)/shard_map/ppermute | solution.py:19
  65.6 87.4 %copy-start = (f32[3,768,128]{1,2,0:T(8,128)}, f32[3,768,128]{1,2,0:T(8,128)S(1)}, u32[]{:S(2)}) copy-start(f32[3,768,128]{1,2,0:T(8,128)S(1)} %multiply_add_fusion.1) | copy-start | bytes 3538948
  66.6 16.2 %all-to-all-start = ((bf16[16,48,128]{2,1,0:T(8,128)(2,1)}), bf16[16,48,128]{2,1,0:T(8,128)(2,1)S(1)}, u32[]{:S(2)}, u32[]{:S(2)}) async-start(bf16[16,48,128]{2,1,0:T(8,128)(2,1)} %bitcast.5), calls=%async_computation | async-start | bytes 393216 | tf_op jit(solution)/shard_map/all_to_all | solution.py:230
  73.9 62.2 %copy-start.152 = (f32[48]{0:T(128)}, f32[48]{0:T(128)S(1)}, u32[]{:S(2)}) copy-start(f32[48]{0:T(128)S(1)} %fusion.516) | copy-start | bytes 580
  137.0 14.1 %all-to-all-start.1 = ((bf16[48,16,128]{2,0,1:T(8,128)(2,1)}), bf16[48,16,128]{2,0,1:T(8,128)(2,1)S(1)}, u32[]{:S(2)}, u32[]{:S(2)}) async-start(bf16[48,16,128]{2,0,1:T(8,128)(2,1)} %copy_bitcast_fusion.7), calls=%async_computation.1 | async-start | bytes 393216 | tf_op jit(solution)/shard_map/all_to_all | solution.py:233
  163.8 103.3 %copy-start.3 = (f32[128,768]{1,0:T(8,128)}, f32[128,768]{1,0:T(8,128)S(1)}, u32[]{:S(2)}) copy-start(f32[128,768]{1,0:T(8,128)S(1)} %get-tuple-element.143) | copy-start | bytes 1179652
  167.4 9.4 collective-permute-start.1
  180.3 14.8 %all-to-all-start.2 = ((bf16[16,48,128]{2,1,0:T(8,128)(2,1)}), bf16[16,48,128]{2,1,0:T(8,128)(2,1)S(1)}, u32[]{:S(2)}, u32[]{:S(2)}) async-start(bf16[16,48,128]{2,1,0:T(8,128)(2,1)} %bitcast.32), calls=%async_computation.2 | async-start | bytes 393216 | tf_op jit(solution)/shard_map/all_to_all | solution.py:230
  186.2 62.2 %copy-start.154 = (f32[48]{0:T(128)}, f32[48]{0:T(128)S(1)}, u32[]{:S(2)}) copy-start(f32[48]{0:T(128)S(1)} %fusion.517) | copy-start | bytes 580
  195.1 53.3 %copy-start.39 = (bf16[16,48,128]{2,1,0:T(8,128)(2,1)}, bf16[16,48,128]{2,1,0:T(8,128)(2,1)S(1)}, u32[]{:S(2)}) copy-start(bf16[16,48,128]{2,1,0:T(8,128)(2,1)S(1)} %all-to-all-done.2) | copy-start | bytes 589828
  249.3 14.1 %all-to-all-start.3 = ((bf16[48,16,128]{2,0,1:T(8,128)(2,1)}), bf16[48,16,128]{2,0,1:T(8,128)(2,1)S(1)}, u32[]{:S(2)}, u32[]{:S(2)}) async-start(bf16[48,16,128]{2,0,1:T(8,128)(2,1)} %copy_bitcast_fusion.6), calls=%async_computation.3 | async-start | bytes 393216 | tf_op jit(solution)/shard_map/all_to_all | solution.py:233
  366.7 3.1 collective-permute-start.2
  390.5 13.5 %all-to-all-start.6 = ((bf16[16,48,128]{2,1,0:T(8,128)(2,1)}), bf16[16,48,128]{2,1,0:T(8,128)(2,1)}, u32[]{:S(2)}, u32[]{:S(2)}) async-start(bf16[16,48,128]{2,1,0:T(8,128)(2,1)} %bitcast.650), calls=%async_computation.6 | async-start | bytes 393216 | tf_op jit(solution)/shard_map/all_to_all | solution.py:319
  394.9 208.6 %reduce-scatter.17.cloned.1.call-start = ((), (), s32[]{:S(2)}) async-start(), calls=%async_computation.17 | async-start | bytes 5013504 | tf_op jit(solution)/shard_map/reduce_scatter | solution.py:405
  399.5 250.2 %reduce-scatter.15.cloned.1.call-start = ((), (), s32[]{:S(2)}) async-start(), calls=%async_computation.16 | async-start | bytes 15040512 | tf_op jit(solution)/shard_map/reduce_scatter | solution.py:404
  478.3 5.5 collective-permute-start.3
  502.4 348.0 %reduce-scatter.23.cloned.1.call-start = ((), (), s32[]{:S(2)}) async-start(), calls=%async_computation.20 | async-start | bytes 20054016 | tf_op jit(solution)/shard_map/reduce_scatter | solution.py:407
  515.0 534.0 %reduce-scatter.19.cloned.1.call-start = ((), (), s32[]{:S(2)}) async-start(), calls=%async_computation.18 | async-start | bytes 20054016 | tf_op jit(solution)/shard_map/reduce_scatter | solution.py:406
  528.6 535.0 %all-reduce.10.cloned.1.call-start = ((), (), s32[]{:S(2)}) async-start(), calls=%async_computation.24 | async-start | bytes 348160 | tf_op jit(solution)/shard_map/psum | solution.py:426
  603.4 461.6 %reduce-scatter.27.cloned.1.call-start = ((), (), s32[]{:S(2)}) async-start(), calls=%async_computation.22 | async-start | bytes 294912
  605.8 473.8 %reduce-scatter.25.cloned.1.call-start = ((), (), s32[]{:S(2)}) async-start(), calls=%async_computation.21 | async-start | bytes 884736
  656.1 441.1 %reduce-scatter.29.cloned.1.call-start = ((), (), s32[]{:S(2)}) async-start(), calls=%async_computation.23 | async-start | bytes 884736
  856.1 259.4 %reduce-scatter.21.cloned.1.call-start = ((), (), s32[]{:S(2)}) async-start(), calls=%async_computation.19 | async-start | bytes 884736 | tf_op jit(solution)/shard_map/reduce_scatter | solution.py:416
  860.7 190.4 %copy-start.38 = (bf16[16,48,128]{2,1,0:T(8,128)(2,1)S(1)}, bf16[16,48,128]{2,1,0:T(8,128)(2,1)}, u32[]{:S(2)}) copy-start(bf16[16,48,128]{2,1,0:T(8,128)(2,1)} %copy-done.37) | copy-start | bytes 589828
  861.4 190.9 %copy-start.6 = (f32[2048,64]{0,1:T(8,128)S(1)}, f32[2048,64]{0,1:T(8,128)}, u32[]{:S(2)}) copy-start(f32[2048,64]{0,1:T(8,128)} %copy-done.5) | copy-start | bytes 1572868
  861.4 190.9 %copy-start.124 = (f32[48]{0:T(128)S(1)}, f32[48]{0:T(128)}, u32[]{:S(2)}) copy-start(f32[48]{0:T(128)} %copy-done.122) | copy-start | bytes 580
  861.4 190.9 %copy-start.127 = (f32[48]{0:T(128)S(1)}, f32[48]{0:T(128)}, u32[]{:S(2)}) copy-start(f32[48]{0:T(128)} %copy-done.125) | copy-start | bytes 580
  861.4 201.3 %copy-start.43 = (bf16[1,128,768]{2,1,0:T(8,128)(2,1)S(1)}, bf16[1,128,768]{2,1,0:T(8,128)(2,1)}, u32[]{:S(2)}) copy-start(bf16[1,128,768]{2,1,0:T(8,128)(2,1)} %param.14) | copy-start | bytes 589828
  861.4 201.3 %copy-start.54 = (f32[128,768]{1,0:T(8,128)S(1)}, f32[128,768]{1,0:T(8,128)}, u32[]{:S(2)}) copy-start(f32[128,768]{1,0:T(8,128)} %get-tuple-element.88) | copy-start | bytes 1179652
  861.4 201.3 %copy-start.92 = (f32[128,768]{1,0:T(8,128)S(1)}, f32[128,768]{1,0:T(8,128)}, u32[]{:S(2)}) copy-start(f32[128,768]{1,0:T(8,128)} %get-tuple-element.156) | copy-start | bytes 1179652
  861.5 201.3 %copy-start.141 = (f32[128]{0:T(128)S(1)}, f32[128]{0:T(128)}, u32[]{:S(2)}) copy-start(f32[128]{0:T(128)} %copy-done.139) | copy-start | bytes 1540
  861.5 201.3 %copy-start.151 = (f32[128]{0:T(128)S(1)}, f32[128]{0:T(128)}, u32[]{:S(2)}) copy-start(f32[128]{0:T(128)} %copy-done.149) | copy-start | bytes 1540
  (157 other events, 994.1 us)
Sparse Core Ops, SparseCore 0:
  399.6 79.3 reduce-scatter.16
  502.5 147.1 reduce-scatter.14
  654.4 195.9 reduce-scatter.22
  854.9 194.0 reduce-scatter.18
  1051.1 10.3 reduce-scatter.26
  1064.3 15.2 reduce-scatter.24
  1081.9 15.2 reduce-scatter.28
  1100.1 15.2 reduce-scatter.20
Sparse Core Ops, SparseCore 1:
  603.5 205.3 all-reduce.9
where the time goes:
time: 1140 us; the launch traced here: 1130 us
  waiting for transfers between devices  487 us (43%)
  matrix products  412 us (36%)
  other arithmetic  72.3 us (6%)
  local copies, waits for them, and re-layouts  52.6 us (5%)
  blocking collectives  49.2 us (4%)
  starting transfers between devices  35.5 us (3%)
  between operations  19.4 us (2%)
    dot_general x88, matrix products, high_einsum(): return jnp.einsum(form, left, right, precision=HIGHEST)  349 us
    reduce_scatter x1, waiting for transfers between devices, body(): lax.psum_scatter(stacked_large[3], 'seq', scatter_dimension=1, tiled=True)  194 us
    reduce_scatter x1, waiting for transfers between devices, body(): lax.psum_scatter(stacked_large[2], 'seq', scatter_dimension=1, tiled=True)  187 us
    dot_general x24, matrix products, low_einsum(): return jnp.einsum(form, left, right, preferred_element_type=jnp.float32)  62.7 us
    reduce_scatter x1, waiting for transfers between devices, body(): lax.psum_scatter(stacked_large[0], 'seq', scatter_dimension=1, tiled=True)  43.9 us
    unnamed x371, local copies, waits for them, and re-layouts  34.4 us
    another operation x4, other arithmetic, body(): jnp.stack([large_all[level][member] for level in range(layer_count)])  31.5 us
    unnamed x12, waiting for transfers between devices  27.7 us
  transfers between devices with their start and end apart: 18, of which 12 were waited for; matrix products, arithmetic and copies ran while one was open for 26% of the time, Pallas kernels for 0%

commit v1 on v0

--- a/solution.py
+++ b/solution.py
@@ -1,8 +1,13 @@
+import functools
 import math
 
 import jax
 import jax.numpy as jnp
+import ml_dtypes
+import numpy as np
 from jax import lax
+from jax.experimental import pallas as pl
+from jax.experimental.pallas import tpu as pltpu
 from jax.sharding import PartitionSpec as P
 
 FEATS = 33
@@ -190,6 +195,386 @@
     )
     g_skip = jnp.sum(d_signal * gated.astype(jnp.float32), axis=1)
     return (d_gated, d_response, g_skip)
+
+
+def unit(k,n):
+    k%=n
+    if (4*k)%n==0:
+        q=(4*k)//n
+        return [(1.0,0.0),(0.0,-1.0),(-1.0,0.0),(0.0,1.0)][q]
+    a=-2.0*math.pi*k/n
+    return (math.cos(a),math.sin(a))
+def times(z,w):
+    re,im=z; c,s=w
+    if s==0.0: return (re,im) if c==1.0 else (-re,-im)
+    if c==0.0: return (-im,re) if s==1.0 else (im,-re)
+    return (re*c-im*s, re*s+im*c)
+def plus(a,b): return (a[0]+b[0],a[1]+b[1])
+def minus(a,b): return (a[0]-b[0],a[1]-b[1])
+def complex_dft(zs,sign):
+    n=len(zs)
+    if n==1: return zs
+    ev=complex_dft(zs[0::2],sign); od=complex_dft(zs[1::2],sign)
+    lo,hi=[],[]
+    for k in range(n//2):
+        v=times(od[k],unit(sign*k,n))
+        lo.append(plus(ev[k],v)); hi.append(minus(ev[k],v))
+    return lo+hi
+def odd_bins(xs):
+    n=len(xs); h=n//2; N=2*n
+    zs=[times((xs[j],-xs[j+h]),unit(j,N)) for j in range(h)]
+    bins={}
+    for q,z in enumerate(complex_dft(zs,1)):
+        k=4*q+1
+        if k<=n: bins[k]=z
+        else: bins[N-k]=(z[0],-z[1])
+    return bins
+def real_bins(xs):
+    n=len(xs)
+    if n==1: return {0:(xs[0],None)}
+    if n==2: return {0:(xs[0]+xs[1],None),1:(xs[0]-xs[1],None)}
+    h=n//2
+    bins={2*k:z for k,z in real_bins([xs[j]+xs[j+h] for j in range(h)]).items()}
+    bins.update(odd_bins([xs[j]-xs[j+h] for j in range(h)]))
+    return bins
+def padded_bins(xs):
+    bins={2*k:z for k,z in real_bins(xs).items()}
+    bins.update(odd_bins(xs))
+    return bins
+def odd_back(bins,n):
+    h=n//2; N=2*n
+    zs=[]
+    for q in range(h):
+        k=4*q+1
+        if k<=n: zs.append(bins[k])
+        else:
+            re,im=bins[N-k]; zs.append((re,-im))
+    vs=[times(z,unit(-j,N)) for j,z in enumerate(complex_dft(zs,-1))]
+    return [v[0] for v in vs]+[-v[1] for v in vs]
+def real_back(bins,n):
+    if n==1: return [bins[0][0]]
+    if n==2: return [bins[0][0]+bins[1][0],bins[0][0]-bins[1][0]]
+    h=n//2
+    ev=real_back({k//2:z for k,z in bins.items() if k%2==0},h)
+    od=odd_back(bins,h)
+    return [ev[j]+od[j] for j in range(h)]+[ev[j]-od[j] for j in range(h)]
+def padded_back(bins,n):
+    ev=real_back({k//2:z for k,z in bins.items() if k%2==0},n)
+    od=odd_back(bins,n)
+    return [a+b for a,b in zip(ev,od)]
+
+
+def turn_table(shards, rows):
+    total = 2 * shards * rows
+    early = np.arange(rows)[None, :, None]
+    late = np.arange(rows)[None, None, :]
+    bins = np.arange(shards + 1)[:, None, None]
+    angle = (early * (bins + 2 * shards * late) % total) * (2.0 * np.pi / total)
+    cos, sin = np.cos(angle), np.sin(angle)
+    top = np.concatenate([cos, -sin], axis=2)
+    bottom = np.concatenate([sin, cos], axis=2)
+    return jnp.asarray(np.concatenate([top, bottom], axis=1).astype(ml_dtypes.bfloat16))
+
+
+def position_table(length):
+    count = (FEATS - 1) // 2
+    steps = np.arange(length)[None, :]
+    angle = (steps * np.arange(1, count + 1)[:, None] % length) * (2.0 * np.pi / length)
+    table = np.concatenate([steps / length, np.cos(angle), np.sin(angle)], axis=0)
+    return jnp.asarray(table.astype(np.float32))
+
+
+def chunks_of(channels):
+    step = 16 if channels % 16 == 0 else channels
+    return [slice(at, at + step) for at in range(0, channels, step)]
+
+
+def load_bins(blocks, bins_ref, chunk):
+    lanes = blocks[0].shape[-1]
+    for k, (re, im) in padded_bins(blocks).items():
+        im = jnp.zeros_like(re) if im is None else im
+        bins_ref[k, chunk, :lanes] = re.astype(jnp.bfloat16)
+        bins_ref[k, chunk, lanes:] = im.astype(jnp.bfloat16)
+
+
+def fold_bins(back_ref, chunk, count, lanes):
+    bins = {
+        k: (back_ref[k, chunk, :lanes], back_ref[k, chunk, lanes:]) for k in range(count + 1)
+    }
+    return padded_back(bins, count)
+
+
+def bin_scale(k, shards, rows):
+    total = 2 * shards * rows
+    return (1.0 if k in (0, shards) else 2.0) / total
+
+
+def bin_product(left, right, conjugate):
+    lanes = left.shape[1] // 2
+    a, b = left[:, :lanes], left[:, lanes:]
+    c, d = right[:, :lanes], right[:, lanes:]
+    if conjugate:
+        return jnp.concatenate([a * c + b * d, b * c - a * d], axis=1)
+    return jnp.concatenate([a * c - b * d, a * d + b * c], axis=1)
+
+
+def turn(left, table):
+    return jnp.dot(left, table, preferred_element_type=jnp.float32)
+
+
+def turn_back(left, table):
+    return lax.dot_general(
+        left.astype(jnp.bfloat16),
+        table,
+        (((1,), (1,)), ((), ())),
+        preferred_element_type=jnp.float32,
+    )
+
+
+def sin_cos(angle):
+    steps = jnp.floor(angle * (2.0 / math.pi) + 0.5)
+    rest = angle - steps * 1.5703125
+    rest = rest - steps * 4.837512969970703e-4
+    rest = rest - steps * 7.549789954891882e-8
+    square = rest * rest
+    sin = rest + rest * square * (
+        -1.6666654611e-1 + square * (8.3321608736e-3 + square * -1.9515295891e-4)
+    )
+    cos = (
+        1.0
+        - 0.5 * square
+        + square
+        * square
+        * (4.166664568298827e-2 + square * (-1.388731625493765e-3 + square * 2.443315711809948e-5))
+    )
+    quarter = steps.astype(jnp.int32)
+    odd = (quarter & 1) == 1
+    sin_out = jnp.where(odd, cos, sin)
+    cos_out = jnp.where(odd, sin, cos)
+    sin_out = jnp.where((quarter & 2) == 2, -sin_out, sin_out)
+    cos_out = jnp.where(((quarter + 1) & 2) == 2, -cos_out, cos_out)
+    return sin_out, cos_out
+
+
+def across(left, right, left_side, right_side):
+    return lax.dot_general(
+        left,
+        right,
+        (((left_side,), (right_side,)), ((), ())),
+        precision=HIGHEST,
+        preferred_element_type=jnp.float32,
+    )
+
+
+def filter_network_kernel(
+    feature_ref,
+    first_ref,
+    middle_ref,
+    last_ref,
+    rate_ref,
+    table_ref,
+    spec_ref,
+    one_ref,
+    slope_one_ref,
+    two_ref,
+    slope_two_ref,
+    window_ref,
+    raw_ref,
+    bins_ref,
+):
+    shards, channels, rows = window_ref.shape
+    one, slope_one = sin_cos(across(first_ref[...], feature_ref[...], 0, 0))
+    one_ref[...] = one
+    slope_one_ref[...] = slope_one
+    two, slope_two = sin_cos(across(middle_ref[...], one, 0, 0))
+    two_ref[...] = two
+    slope_two_ref[...] = slope_two
+    raw_ref[...] = across(last_ref[...], two, 0, 0)
+    rate = rate_ref[...]
+    size = jnp.sqrt(rate + 1.0 / (shards * rows))
+    step = lax.broadcasted_iota(jnp.int32, (channels, rows), 1)
+    for j in range(shards):
+        window = jnp.exp(-rate * (step + j * rows).astype(jnp.float32)) * size
+        window_ref[j] = window
+        at = slice(j * rows, (j + 1) * rows)
+        raw_ref[:, at] = raw_ref[:, at] * window
+    for chunk in chunks_of(channels):
+        load_bins(
+            [raw_ref[chunk, j * rows : (j + 1) * rows] for j in range(shards)], bins_ref, chunk
+        )
+    for k in range(shards + 1):
+        spec_ref[k] = turn(bins_ref[k], table_ref[k]) * bin_scale(k, shards, rows)
+
+
+def filter_network(features, first, middle, last, rates, table):
+    hidden, channels = last.shape
+    length = features.shape[1]
+    bins, span, _ = table.shape
+    rows = span // 2
+    shards = length // rows
+    wide = jax.ShapeDtypeStruct((hidden, length), jnp.float32)
+    return pl.pallas_call(
+        filter_network_kernel,
+        out_shape=[
+            jax.ShapeDtypeStruct((bins, channels, span), jnp.float32),
+            wide,
+            wide,
+            wide,
+            wide,
+            jax.ShapeDtypeStruct((shards, channels, rows), jnp.float32),
+        ],
+        scratch_shapes=[
+            pltpu.VMEM((channels, length), jnp.float32),
+            pltpu.VMEM((bins, channels, span), jnp.bfloat16),
+        ],
+        compiler_params=pltpu.CompilerParams(vmem_limit_bytes=40 << 20),
+        name="filter_network",
+    )(features, first, middle, last, rates, table)
+
+
+def conv_forward_kernel(
+    gated_ref, filter_ref, skip_ref, table_ref, conv_ref, spec_ref, bins_ref, back_ref
+):
+    shards, channels, rows = gated_ref.shape
+    for chunk in chunks_of(channels):
+        load_bins(
+            [gated_ref[j, chunk].astype(jnp.float32) for j in range(shards)], bins_ref, chunk
+        )
+    for k in range(shards + 1):
+        spec = turn(bins_ref[k], table_ref[k])
+        spec_ref[k] = spec.astype(jnp.bfloat16)
+        back_ref[k] = turn_back(bin_product(spec, filter_ref[k], False), table_ref[k])
+    for chunk in chunks_of(channels):
+        skip = skip_ref[chunk]
+        for j, block in enumerate(fold_bins(back_ref, chunk, shards, rows)):
+            conv = block + skip * gated_ref[j, chunk].astype(jnp.float32)
+            conv_ref[j, chunk] = conv.astype(jnp.bfloat16)
+
+
+def conv_backward_kernel(
+    gated_ref, filter_ref, skip_ref, table_ref, conv_ref, spec_ref, bins_ref, back_ref
+):
+    shards, channels, rows = gated_ref.shape
+    for chunk in chunks_of(channels):
+        load_bins(
+            [gated_ref[j, chunk].astype(jnp.float32) for j in range(shards)], bins_ref, chunk
+        )
+    for k in range(shards + 1):
+        spec = turn(bins_ref[k], table_ref[k])
+        spec_ref[k] = spec.astype(jnp.bfloat16)
+        back_ref[k] = turn_back(bin_product(spec, filter_ref[k], True), table_ref[k])
+    for chunk in chunks_of(channels):
+        skip = skip_ref[chunk]
+        for j, block in enumerate(fold_bins(back_ref, chunk, shards, rows)):
+            conv = block + skip * gated_ref[j, chunk].astype(jnp.float32)
+            conv_ref[j, chunk] = conv.astype(jnp.bfloat16)
+
+
+def conv_call(kernel, name, gated, filter_spec, skip, table):
+    bins, channels, span = filter_spec.shape
+    return pl.pallas_call(
+        kernel,
+        out_shape=[
+            jax.ShapeDtypeStruct(gated.shape, jnp.bfloat16),
+            jax.ShapeDtypeStruct((bins, channels, span), jnp.bfloat16),
+        ],
+        scratch_shapes=[
+            pltpu.VMEM((bins, channels, span), jnp.bfloat16),
+            pltpu.VMEM((bins, channels, span), jnp.float32),
+        ],
+        compiler_params=pltpu.CompilerParams(vmem_limit_bytes=40 << 20),
+        name=name,
+    )(gated, filter_spec, skip, table)
+
+
+def conv_forward(gated, filter_spec, skip, table):
+    return conv_call(conv_forward_kernel, "conv_forward", gated, filter_spec, skip, table)
+
+
+def conv_backward(d_conv, filter_spec, skip, table):
+    return conv_call(conv_backward_kernel, "conv_backward", d_conv, filter_spec, skip, table)
+
+
+def filter_back_kernel(
+    d_spec_ref,
+    spec_ref,
+    d_conv_ref,
+    gated_ref,
+    feature_ref,
+    middle_ref,
+    last_ref,
+    one_ref,
+    slope_one_ref,
+    two_ref,
+    slope_two_ref,
+    window_ref,
+    table_ref,
+    g_first_ref,
+    g_middle_ref,
+    g_last_ref,
+    g_skip_ref,
+    back_ref,
+    raw_ref,
+):
+    shards, channels, rows = d_conv_ref.shape
+    for k in range(shards + 1):
+        spec = bin_product(
+            d_spec_ref[k].astype(jnp.float32), spec_ref[k].astype(jnp.float32), True
+        )
+        back_ref[k] = turn_back(spec * bin_scale(k, shards, rows), table_ref[k])
+    for chunk in chunks_of(channels):
+        total = None
+        for j, block in enumerate(fold_bins(back_ref, chunk, shards, rows)):
+            raw_ref[chunk, j * rows : (j + 1) * rows] = block * window_ref[j, chunk]
+            term = d_conv_ref[j, chunk].astype(jnp.float32) * gated_ref[j, chunk].astype(
+                jnp.float32
+            )
+            total = term if total is None else total + term
+        g_skip_ref[chunk] = jnp.sum(total, axis=1, keepdims=True)
+    d_raw = raw_ref[...]
+    g_last_ref[...] = across(two_ref[...], d_raw, 1, 1)
+    d_two = across(last_ref[...], d_raw, 1, 0) * slope_two_ref[...]
+    g_middle_ref[...] = across(one_ref[...], d_two, 1, 1)
+    d_one = across(middle_ref[...], d_two, 1, 0) * slope_one_ref[...]
+    g_first_ref[...] = across(feature_ref[...], d_one, 1, 1)
+
+
+def filter_network_back(
+    d_spec, spec, d_conv, gated, features, middle, last, kept, table
+):
+    _, one, slope_one, two, slope_two, window = kept
+    bins, channels, span = spec.shape
+    hidden, length = one.shape
+    feats = features.shape[0]
+    return pl.pallas_call(
+        filter_back_kernel,
+        out_shape=[
+            jax.ShapeDtypeStruct((feats, hidden), jnp.float32),
+            jax.ShapeDtypeStruct((hidden, hidden), jnp.float32),
+            jax.ShapeDtypeStruct((hidden, channels), jnp.float32),
+            jax.ShapeDtypeStruct((channels, 1), jnp.float32),
+        ],
+        scratch_shapes=[
+            pltpu.VMEM((bins, channels, span), jnp.float32),
+            pltpu.VMEM((channels, length), jnp.float32),
+        ],
+        compiler_params=pltpu.CompilerParams(vmem_limit_bytes=40 << 20),
+        name="filter_network_back",
+    )(
+        d_spec,
+        spec,
+        d_conv,
+        gated,
+        features,
+        middle,
+        last,
+        one,
+        slope_one,
+        two,
+        slope_two,
+        window,
+        table,
+    )
 
 
 def layer_forward(state, weights, setting):
@@ -217,20 +602,24 @@
     last_columns = lax.dynamic_slice_in_dim(last, offset, channels, 1)
     skip_columns = lax.dynamic_slice_in_dim(skip, offset, channels, 0)
     rate_columns = lax.dynamic_slice_in_dim(rates, offset, channels, 0)
-    response, filter_kept = filter_forward(
-        features, first, middle, last_columns, rate_columns, length
-    )
-    filter_real, filter_imag = forward_transform(response, tables)
+    filter_kept = filter_network(
+        features, first, middle, last_columns, rate_columns[:, None], tables
+    )
+    filter_spec = filter_kept[0]
     taps = short_taps.reshape(3, 3, width)
     edge = from_behind(projected[:, :, rows - 2 :], "seq", 1)
     extended = jnp.concatenate([edge, projected], axis=2).astype(jnp.float32)
     tap_use = taps[:, :, :, None]
     shorted = short_forward(extended, tap_use)
     gated_rows = to_low(shorted[2] * shorted[1])
-    gated = lax.all_to_all(gated_rows, "seq", split_axis=0, concat_axis=1, tiled=True)
-    conv, signal_spec = long_forward(gated, filter_real, filter_imag, skip_columns, tables)
-    conv_low = to_low(conv)
-    conv_here = lax.all_to_all(conv_low, "seq", split_axis=1, concat_axis=0, tiled=True)
+    shards = length // rows
+    gated = lax.all_to_all(
+        gated_rows.reshape(shards, channels, rows), "seq", split_axis=0, concat_axis=0, tiled=True
+    )
+    conv_low, signal_spec = conv_forward(gated, filter_spec, skip_columns[:, None], tables)
+    conv_here = lax.all_to_all(
+        conv_low, "seq", split_axis=0, concat_axis=0, tiled=True
+    ).reshape(width, rows)
     mixed = to_low(conv_here.astype(jnp.float32) * shorted[0])
     middle_state = state + low_einsum("ct,ce->te", mixed, out_proj)
     normed_mlp, scale_mlp = normalize(middle_state)
@@ -248,8 +637,7 @@
         conv_here,
         mixed,
         filter_kept,
-        filter_real,
-        filter_imag,
+        filter_spec,
         signal_spec,
         normed_mlp,
         scale_mlp,
@@ -289,8 +677,7 @@
         conv_here,
         mixed,
         filter_kept,
-        filter_real,
-        filter_imag,
+        filter_spec,
         signal_spec,
         normed_mlp,
         scale_mlp,
@@ -316,21 +703,23 @@
     d_mixed_wide = d_mixed.astype(jnp.float32)
     d_conv_rows = to_low(d_mixed_wide * shorted[0])
     d_zero = d_mixed_wide * conv_here.astype(jnp.float32)
-    d_conv = lax.all_to_all(d_conv_rows, "seq", split_axis=0, concat_axis=1, tiled=True)
-    d_gated, d_response, g_skip = long_backward(
-        d_conv, gated, filter_real, filter_imag, skip_columns, signal_spec, tables
-    )
+    shards, channels, _ = gated.shape
+    d_conv = lax.all_to_all(
+        d_conv_rows.reshape(gated.shape), "seq", split_axis=0, concat_axis=0, tiled=True
+    )
+    d_gated, d_spec = conv_backward(d_conv, filter_spec, skip_columns[:, None], tables)
     d_gated_rows = lax.all_to_all(
-        to_low(d_gated), "seq", split_axis=1, concat_axis=0, tiled=True
-    ).astype(jnp.float32)
+        d_gated, "seq", split_axis=0, concat_axis=0, tiled=True
+    ).reshape(width, rows).astype(jnp.float32)
     d_shorted = jnp.stack([d_zero, d_gated_rows * shorted[2], d_gated_rows * shorted[1]])
     after = from_behind(d_shorted[:, :, :2], "seq", -1)
     d_extended = jnp.concatenate([d_shorted, after], axis=2)
     d_projected = to_low(short_backward(d_extended, tap_use))
     g_taps = tap_grads(d_shorted, extended)
-    g_first, g_middle, g_last = filter_backward(
-        d_response, features, middle, last_columns, filter_kept
-    )
+    g_first, g_middle, g_last, g_skip = filter_network_back(
+        d_spec, signal_spec, d_conv, gated, features, middle, last_columns, filter_kept, tables
+    )
+    g_skip = g_skip[:, 0]
     d_flat = d_projected.reshape(3 * width, rows)
     g_in = low_einsum("td,ct->dc", u_mix, d_flat)
     d_u_mix = low_einsum("ct,dc->td", d_flat, in_proj)
@@ -364,7 +753,7 @@
     shards = lax.axis_size("seq")
     length = rows * shards
     offset = lax.axis_index("seq") * (width // shards)
-    setting = (position_features(length), transform_tables(length, FFT_COLS), offset)
+    setting = (position_table(length), turn_table(shards, rows), offset)
     stacks = (
         mix_gain,
         in_proj,

time: 1140 us -> 928 us (0.81)
  matrix products: 412 us -> 66.5 us
  waiting for transfers between devices: 487 us -> 551 us
  local copies, waits for them, and re-layouts: 52.6 us -> 97.8 us
  Pallas kernels: 0 us -> 24 us
    dot_general x88 -> x0, matrix products: 349 us -> none  [high_einsum(): return jnp.einsum(form, left, right, precision=HIGHEST)]
    reduce_scatter x1, waiting for transfers between devices: 43.9 us -> 100 us  [body(): lax.psum_scatter(stacked_large[0], 'seq', scatter_dimension=1, tiled=True)]
    unnamed x371 -> x338, local copies, waits for them, and re-layouts: 34.4 us -> 65.1 us
    pallas_call x0 -> x8, Pallas kernels: none -> 24 us  [the longest x2 9.48 us: filter_network_back(): pl.pallas_call(filter_back_kernel, out_shape=[jax.ShapeDtypeStruct((feats...]
    all_to_all x3 -> x4, blocking collectives: 39.5 us -> 48.9 us  [the longest x2 25.7 us: layer_backward(): lax.all_to_all(d_conv_rows.reshape(gated.shape), 'seq', split_axis=0, con...]
    all_to_all x5 -> x4, starting transfers between devices: 27.7 us -> 23.7 us  [the longest x2 12.9 us: layer_forward(): lax.all_to_all(gated_rows.reshape(shards, channels, rows), 'seq', split_a...]
  transfers between devices with their start and end apart: 18 -> 17, of which waited for: 12 -> 9; matrix products, arithmetic and copies ran while one was open for 26% -> 11% of each run, Pallas kernels for 0% -> 2%
where the time goes in v1:
time: 928 us; the launch traced here: 916 us
  waiting for transfers between devices  551 us (59%)
  local copies, waits for them, and re-layouts  97.8 us (11%)
  other arithmetic  68.8 us (7%)
  matrix products  66.5 us (7%)
  blocking collectives  58.3 us (6%)
  starting transfers between devices  32.4 us (3%)
  Pallas kernels  24 us (3%)
  between operations  17.8 us (2%)
    reduce_scatter x1, waiting for transfers between devices, body(): lax.psum_scatter(stacked_large[2], 'seq', scatter_dimension=1, tiled=True)  195 us
    reduce_scatter x1, waiting for transfers between devices, body(): lax.psum_scatter(stacked_large[3], 'seq', scatter_dimension=1, tiled=True)  195 us
    reduce_scatter x1, waiting for transfers between devices, body(): lax.psum_scatter(stacked_large[0], 'seq', scatter_dimension=1, tiled=True)  100 us
    dot_general x24, matrix products, low_einsum(): return jnp.einsum(form, left, right, preferred_element_type=jnp.float32)  66.5 us
    unnamed x338, local copies, waits for them, and re-layouts  65.1 us
    another operation x4, other arithmetic, body(): jnp.stack([large_all[level][member] for level in range(layer_count)])  27.2 us
    unnamed x12, waiting for transfers between devices  26.2 us
    all_to_all x2, blocking collectives, layer_backward(): lax.all_to_all(d_conv_rows.reshape(gated.shape), 'seq', split_axis=0, con...  25.7 us
  transfers between devices with their start and end apart: 17, of which 9 were waited for; matrix products, arithmetic and copies ran while one was open for 11% of the time, Pallas kernels for 2%

profile of v1, /device:TPU:0, one launch (start us, length us, event | category | flops | bytes accessed | tf_op | source)
XLA Modules:
  0.0 916.4 jit_solution(9911690265573519198)
XLA Ops:
  25.0 7.3 all-to-all-start
  45.5 4.9 all-to-all-start.1
  51.0 8.4 all-to-all-done.1
  66.4 4.8 multiply_convert_fusion.1
  71.2 3.5 fusion.128
  92.0 5.7 all-to-all-start.2
  114.7 5.9 all-to-all-start.3
  120.6 9.0 all-to-all-done.3
  137.3 4.6 multiply_convert_fusion
  141.9 4.3 fusion.53
  153.7 12.6 %all_to_all.40.gated_ref.d_conv_ref = bf16[16,48,128]{2,1,0:T(8,128)(2,1)S(1)} all-to-all(bf16[16,48,128]{2,1,0:T(8,128)(2,1)} %bitcast.271), channel_id=1, replica_groups=mesh['dp'=2,'seq'=16] {'seq'}, dimensions={0} | all-to-all | bytes 393216 | tf_op jit(solution)/shard_map/all_to_all | solution.py:707
  170.0 11.6 %all_to_all.41 = bf16[16,48,128]{2,1,0:T(8,128)(2,1)S(1)} all-to-all(bf16[16,48,128]{2,1,0:T(8,128)(2,1)S(1)} %get-tuple-element.45), channel_id=1, replica_groups=mesh['dp'=2,'seq'=16] {'seq'}, dimensions={0} | all-to-all | bytes 393216 | tf_op jit(solution)/shard_map/all_to_all | solution.py:711
  194.8 4.4 multiply_reduce_fusion.8
  200.7 4.5 fusion.46
  218.5 13.1 %all_to_all.42.gated_ref.d_conv_ref = bf16[16,48,128]{2,1,0:T(8,128)(2,1)S(1)} all-to-all(bf16[16,48,128]{2,1,0:T(8,128)(2,1)} %bitcast.272), channel_id=1, replica_groups=mesh['dp'=2,'seq'=16] {'seq'}, dimensions={0} | all-to-all | bytes 393216 | tf_op jit(solution)/shard_map/all_to_all | solution.py:707
  234.1 11.6 %all_to_all.43 = bf16[16,48,128]{2,1,0:T(8,128)(2,1)S(1)} all-to-all(bf16[16,48,128]{2,1,0:T(8,128)(2,1)S(1)} %get-tuple-element.46), channel_id=1, replica_groups=mesh['dp'=2,'seq'=16] {'seq'}, dimensions={0} | all-to-all | bytes 393216 | tf_op jit(solution)/shard_map/all_to_all | solution.py:711
  249.7 4.0 convolution_bitcast_fusion.4
  258.6 4.0 convolution_bitcast_fusion.5
  262.6 11.1 %pad_maximum_fusion.2 = f32[2,768,2304]{2,1,0:T(8,128)} fusion(f32[1,768,2304]{2,1,0:T(8,128)} %convolution_bitcast_fusion.4, f32[1,768,2304]{2,1,0:T(8,128)} %convolution_bitcast_fusion.5), kind=kLoop, calls=%fused_computation.2 | loop fusion | flops 3538944 | bytes 28311552 | tf_op jit(solution)/shard_map/stack | solution.py:790
  278.7 6.7 pad_maximum_fusion.1
  290.4 7.0 pad_maximum_fusion
  307.2 4.8 filter_network_back.3
  324.9 4.7 filter_network_back.2
  330.9 3.5 fusion.108
  338.2 100.4 %reduce-scatter.15.cloned.1.call-done = f32[2,48,2304]{2,1,0:T(8,128)} async-done(((f32[2,768,2304]{2,1,0:T(8,128)}), f32[2,48,2304]{2,1,0:T(8,128)}) %reduce-scatter.15.cloned.1.call-update) | async-done | bytes 884752 | tf_op jit(solution)/shard_map/reduce_scatter | solution.py:793
  443.0 195.1 %reduce-scatter.23.cloned.1.call-done = f32[2,192,768]{2,1,0:T(8,128)} async-done(((f32[2,3072,768]{2,1,0:T(8,128)}), f32[2,192,768]{2,1,0:T(8,128)}) %reduce-scatter.23.cloned.1.call-update) | async-done | bytes 1179664 | tf_op jit(solution)/shard_map/reduce_scatter | solution.py:796
  641.5 195.1 %reduce-scatter.19.cloned.1.call-done = f32[2,48,3072]{2,1,0:T(8,128)} async-done(((f32[2,768,3072]{2,1,0:T(8,128)}), f32[2,48,3072]{2,1,0:T(8,128)}) %reduce-scatter.19.cloned.1.call-update) | async-done | bytes 1179664 | tf_op jit(solution)/shard_map/reduce_scatter | solution.py:795
  838.8 4.0 fusion.64
  843.1 9.4 %all-reduce.1 = (f32[2,64,48]{2,1,0:T(8,128)S(1)}, f32[2,48]{1,0:T(2,128)}) all-reduce(f32[2,64,48]{2,1,0:T(8,128)S(1)} %pad_maximum_fusion.9, f32[2,48]{1,0:T(2,128)S(1)} %pad_maximum_fusion.13), channel_id=1, replica_groups=mesh['dp'=2,'seq'=16] {'dp'}, use_global_device_ids=true, to_apply=%region_30.0 | all-reduce | flops 6240 | bytes 49920 | tf_op jit(solution)/shard_map/psum | solution.py:821
  857.4 11.1 %reduce-scatter.25.cloned.1.call-done = bf16[1152,96]{1,0:T(8,128)(2,1)} async-done(((bf16[2304,96]{1,0:T(8,128)(2,1)}), bf16[1152,96]{1,0:T(8,128)(2,1)}) %reduce-scatter.25.cloned.1.call-update) | async-done | bytes 221200
  871.1 14.9 %reduce-scatter.29.cloned.1.call-done = bf16[384,384]{1,0:T(8,128)(2,1)} async-done(((bf16[768,384]{1,0:T(8,128)(2,1)}), bf16[384,384]{1,0:T(8,128)(2,1)}) %reduce-scatter.29.cloned.1.call-update) | async-done | bytes 294928
  888.9 15.4 %reduce-scatter.21.cloned.1.call-done = bf16[2,48,1536]{2,1,0:T(8,128)(2,1)} async-done(((bf16[2,48,3072]{2,1,0:T(8,128)(2,1)}), bf16[2,48,1536]{2,1,0:T(8,128)(2,1)}) %reduce-scatter.21.cloned.1.call-update) | async-done | bytes 294928 | tf_op jit(solution)/shard_map/reduce_scatter | solution.py:805
  (513 shorter events, 191.3 us)
Async XLA Ops:
  8.8 66.2 %copy-start.125 = (f32[768]{0:T(1024)}, f32[768]{0:T(1024)S(1)}, u32[]{:S(2)}) copy-start(f32[768]{0:T(1024)S(1)} %get-tuple-element.134) | copy-start | bytes 9220
  16.1 5.7 collective-permute-start
  22.0 10.6 %copy-start = (bf16[17,256,256]{2,1,0:T(8,128)(2,1)S(1)}, bf16[17,256,256]{2,1,0:T(8,128)(2,1)}, u32[]{:S(2)}) copy-start(bf16[17,256,256]{2,1,0:T(8,128)(2,1)} %constant.56.clone.table_ref) | copy-start | bytes 6684676
  25.0 16.3 %all-to-all-start = ((bf16[16,48,128]{2,1,0:T(8,128)(2,1)}), bf16[16,48,128]{2,1,0:T(8,128)(2,1)}, u32[]{:S(2)}, u32[]{:S(2)}) async-start(bf16[16,48,128]{2,1,0:T(8,128)(2,1)} %bitcast.5), calls=%async_computation | async-start | bytes 393216 | tf_op jit(solution)/shard_map/all_to_all | solution.py:616
  32.6 67.5 %copy-start.39 = (f32[64,64]{1,0:T(8,128)}, f32[64,64]{1,0:T(8,128)S(1)}, u32[]{:S(2)}) copy-start(f32[64,64]{1,0:T(8,128)S(1)} %get-tuple-element.161.middle_ref) | copy-start | bytes 49156
  45.5 13.9 %all-to-all-start.1 = ((bf16[16,48,128]{2,1,0:T(8,128)(2,1)}), bf16[16,48,128]{2,1,0:T(8,128)(2,1)}, u32[]{:S(2)}, u32[]{:S(2)}) async-start(bf16[16,48,128]{2,1,0:T(8,128)(2,1)} %copy-done.41), calls=%async_computation.1 | async-start | bytes 393216 | tf_op jit(solution)/shard_map/all_to_all | solution.py:620
  51.0 15.2 %copy-start.127 = (f32[768]{0:T(1024)}, f32[768]{0:T(1024)S(1)}, u32[]{:S(2)}) copy-start(f32[768]{0:T(1024)S(1)} %get-tuple-element.133) | copy-start | bytes 9220
  83.5 2.8 collective-permute-start.1
  92.0 17.5 %all-to-all-start.2 = ((bf16[16,48,128]{2,1,0:T(8,128)(2,1)}), bf16[16,48,128]{2,1,0:T(8,128)(2,1)}, u32[]{:S(2)}, u32[]{:S(2)}) async-start(bf16[16,48,128]{2,1,0:T(8,128)(2,1)} %bitcast.270), calls=%async_computation.2 | async-start | bytes 393216 | tf_op jit(solution)/shard_map/all_to_all | solution.py:616
  114.7 15.0 %all-to-all-start.3 = ((bf16[16,48,128]{2,1,0:T(8,128)(2,1)}), bf16[16,48,128]{2,1,0:T(8,128)(2,1)}, u32[]{:S(2)}, u32[]{:S(2)}) async-start(bf16[16,48,128]{2,1,0:T(8,128)(2,1)} %copy-done.42), calls=%async_computation.3 | async-start | bytes 393216 | tf_op jit(solution)/shard_map/all_to_all | solution.py:620
  120.6 215.3 %reduce-scatter.17.cloned.1.call-start = ((), (), s32[]{:S(2)}) async-start(), calls=%async_computation.17 | async-start | bytes 5013504 | tf_op jit(solution)/shard_map/reduce_scatter | solution.py:794
  136.9 11.7 %copy-start.62 = (f32[128,768]{1,0:T(8,128)}, f32[128,768]{1,0:T(8,128)S(1)}, u32[]{:S(2)}) copy-start(f32[128,768]{1,0:T(8,128)S(1)} %get-tuple-element.176) | copy-start | bytes 1179652
  185.8 3.3 collective-permute-start.2
  212.8 225.8 %reduce-scatter.15.cloned.1.call-start = ((), (), s32[]{:S(2)}) async-start(), calls=%async_computation.16 | async-start | bytes 15040512 | tf_op jit(solution)/shard_map/reduce_scatter | solution.py:793
  248.0 5.7 collective-permute-start.3
  273.7 364.4 %reduce-scatter.23.cloned.1.call-start = ((), (), s32[]{:S(2)}) async-start(), calls=%async_computation.20 | async-start | bytes 20054016 | tf_op jit(solution)/shard_map/reduce_scatter | solution.py:796
  285.4 551.2 %reduce-scatter.19.cloned.1.call-start = ((), (), s32[]{:S(2)}) async-start(), calls=%async_computation.18 | async-start | bytes 20054016 | tf_op jit(solution)/shard_map/reduce_scatter | solution.py:795
  297.4 556.7 %all-reduce.4.cloned.1.call-start = ((), (), s32[]{:S(2)}) async-start(), calls=%async_computation.24 | async-start | bytes 348160 | tf_op jit(solution)/shard_map/psum | solution.py:815
  307.2 10.7 %copy-start.8 = (bf16[16,48,128]{2,1,0:T(8,128)(2,1)S(1)}, bf16[16,48,128]{2,1,0:T(8,128)(2,1)}, u32[]{:S(2)}) copy-start(bf16[16,48,128]{2,1,0:T(8,128)(2,1)} %copy-done.7) | copy-start | bytes 589828
  307.2 10.7 %copy-start.10 = (f32[64,2048]{1,0:T(8,128)S(1)}, f32[64,2048]{1,0:T(8,128)}, u32[]{:S(2)}) copy-start(f32[64,2048]{1,0:T(8,128)} %copy-done.9) | copy-start | bytes 1572868
  335.8 519.7 %reduce-scatter.27.cloned.1.call-start = ((), (), s32[]{:S(2)}) async-start(), calls=%async_computation.22 | async-start | bytes 294912
  338.2 530.3 %reduce-scatter.25.cloned.1.call-start = ((), (), s32[]{:S(2)}) async-start(), calls=%async_computation.21 | async-start | bytes 884736
  443.0 443.1 %reduce-scatter.29.cloned.1.call-start = ((), (), s32[]{:S(2)}) async-start(), calls=%async_computation.23 | async-start | bytes 884736
  641.4 197.4 %copy-start.63 = (f32[128,768]{1,0:T(8,128)S(1)}, f32[128,768]{1,0:T(8,128)}, u32[]{:S(2)}) copy-start(f32[128,768]{1,0:T(8,128)} %copy-done.62) | copy-start | bytes 1179652
  641.4 197.4 %copy-start.84 = (bf16[128,3072]{1,0:T(8,128)(2,1)S(1)}, bf16[128,3072]{1,0:T(8,128)(2,1)}, u32[]{:S(2)}) copy-start(bf16[128,3072]{1,0:T(8,128)(2,1)} %get-tuple-element.177) | copy-start | bytes 2359300
  641.4 262.9 %reduce-scatter.21.cloned.1.call-start = ((), (), s32[]{:S(2)}) async-start(), calls=%async_computation.19 | async-start | bytes 884736 | tf_op jit(solution)/shard_map/reduce_scatter | solution.py:805
  838.8 14.4 %copy-start.71 = (bf16[1,128,768]{2,1,0:T(8,128)(2,1)S(1)}, bf16[1,128,768]{2,1,0:T(8,128)(2,1)}, u32[]{:S(2)}) copy-start(bf16[1,128,768]{2,1,0:T(8,128)(2,1)} %param.16) | copy-start | bytes 589828
  838.8 14.4 %copy-start.77 = (f32[128,768]{1,0:T(8,128)S(1)}, f32[128,768]{1,0:T(8,128)}, u32[]{:S(2)}) copy-start(f32[128,768]{1,0:T(8,128)} %get-tuple-element.144) | copy-start | bytes 1179652
  871.1 35.0 %copy-start.135 = (f32[2,768]{1,0:T(2,128)S(1)}, f32[2,768]{1,0:T(2,128)}, u32[]{:S(2)}) copy-start(f32[2,768]{1,0:T(2,128)} %get-tuple-element.189) | copy-start | bytes 18436
  871.1 35.6 %copy-start.116 = (f32[2,3,2304]{2,0,1:T(2,128)S(1)}, f32[2,3,2304]{2,0,1:T(2,128)}, u32[]{:S(2)}) copy-start(f32[2,3,2304]{2,0,1:T(2,128)} %get-tuple-element.191) | copy-start | bytes 165892
  871.1 36.2 %copy-start.115 = (f32[2,64,64]{2,1,0:T(8,128)S(1)}, f32[2,64,64]{2,1,0:T(8,128)}, u32[]{:S(2)}) copy-start(f32[2,64,64]{2,1,0:T(8,128)} %get-tuple-element.193) | copy-start | bytes 98308
  871.1 36.8 %copy-start.134 = (f32[2,768]{1,0:T(2,128)S(1)}, f32[2,768]{1,0:T(2,128)}, u32[]{:S(2)}) copy-start(f32[2,768]{1,0:T(2,128)} %get-tuple-element.197) | copy-start | bytes 18436
  (145 other events, 418.3 us)
Sparse Core Ops, SparseCore 0:
  212.9 75.3 reduce-scatter.16
  293.0 145.5 reduce-scatter.14
  443.3 194.7 reduce-scatter.22
  642.7 193.8 reduce-scatter.18
  839.3 10.7 reduce-scatter.26
  852.9 15.4 reduce-scatter.24
  870.7 15.2 reduce-scatter.28
  889.0 15.2 reduce-scatter.20
Sparse Core Ops, SparseCore 1:
  335.9 233.7 all-reduce.3
